TPU v7x, 128 devices: a whole 4x4x4 slice. The times are simulated.
128 devices in a mesh: sample: 32 (over x, z, core), feature: 4 (over y).
Axes of the slice: x: 4, y: 4, z: 4, core: 2. Of those that a mesh axis runs over, the one named last changes fastest.
Arguments:
- feat_values: float32 [65536, 2048], P('sample', 'feature'), may hold values from -0.6 to 0.6
- block_ids: int32 [512, 16], P('sample', 'feature'), may hold values from 0 to 8191
- fixed_weights: float32 [32768, 128], P('feature'), may hold values from -1.5 to 1.5
- labels: float32 [65536], P('sample'), may hold values from 0 to 1
- prior_scores: float32 [65536], P('sample'), may hold values from -3 to 3
- member_feats: float32 [65536, 128], P(('sample', 'feature')), may hold values from -1.8 to 1.8
- member_ids: int32 [65536], P(('sample', 'feature')), may hold values from 0 to 4095, as said below
- member_coefs: float32 [4096, 128], P(('sample', 'feature')), may hold values from -1.5 to 1.5
Outputs:
- new_weights: float32 [32768, 128], P('feature')
- new_coefs: float32 [4096, 128], P(('sample', 'feature'))
- total_scores: float32 [65536, 1], P(('sample', 'feature'))
Inputs may be any that keep to these rules, and one draw needn't show every extreme that they name: member_ids // 32 is the index along sample+feature of the device that owns the member; no member has more than 32 rows, and every member of some owner has exactly 32; at most 8 rows of one device belong to members of one owner, and every device has exactly 8 rows for some owner.
All inputs are finite; a program needn't handle non-finite values.
Results may differ from a plain program's by a relative error of at most 0.0003.
Values sent between devices are 32-bit elements; how exact they have to be, the bound alone decides.
No kernel may reach another device: no remote copies, remote signals or barrier semaphores. Data moves between devices by JAX's collectives and lax.ppermute only.
A program may use at most 128 MiB of HBM per device.

v0:
```python
import jax
import jax.numpy as jnp
from jax import lax
from jax.sharding import PartitionSpec as P

NEWTON = 2
STEP_SIZE = 0.5
FIXED_RIDGE = 0.1
MEMBER_RIDGE = 1.0
MEMBER_STEP = 0.5
HIGH = lax.Precision.HIGHEST


def partial_margin(tiled, block_ids, weights):
    chosen = weights[block_ids]
    local = jnp.einsum("trkb,tkb->tr", tiled, chosen, precision=HIGH).reshape(-1)
    return lax.psum(local, "feature")


def newton_update(weights, gradient, hessian):
    return weights - STEP_SIZE * (gradient + FIXED_RIDGE * weights) / (hessian + 1.0)


def member_solve(group_feats, weight, gradient_re):
    group = group_feats.shape[1]
    feat_width = group_feats.shape[2]
    scaled = group_feats * jnp.sqrt(weight)[:, :, None]
    small = (
        jnp.einsum("mgf,mhf->mgh", scaled, scaled, precision=HIGH)
        + MEMBER_RIDGE * jnp.eye(group, dtype=jnp.float32)[None]
    )
    projected = jnp.einsum("mgf,mf->mg", scaled, gradient_re, precision=HIGH)
    factor = jnp.linalg.cholesky(small)
    middle = lax.linalg.triangular_solve(factor, projected[:, :, None], left_side=True, lower=True)
    inner = lax.linalg.triangular_solve(
        factor, middle, left_side=True, lower=True, transpose_a=True
    )
    return gradient_re - jnp.einsum("mgf,mg->mf", scaled, inner[:, :, 0], precision=HIGH)


def shards(
    feat_values,
    block_ids,
    fixed_weights,
    labels,
    prior_scores,
    member_feats,
    member_ids,
    member_coefs,
):
    tile_count = block_ids.shape[0]
    slots_tile = block_ids.shape[1]
    block_width = fixed_weights.shape[1]
    shard_blocks = fixed_weights.shape[0]
    tiled = feat_values.reshape(tile_count, -1, slots_tile, block_width)
    margin = partial_margin(tiled, block_ids, fixed_weights)
    probs = jax.nn.sigmoid(margin + prior_scores)
    residual = (probs - labels).reshape(tile_count, -1)
    curvature = (probs * (1.0 - probs)).reshape(tile_count, -1)
    grad_tiles = jnp.einsum("trkb,tr->tkb", tiled, residual, precision=HIGH)
    hess_tiles = jnp.einsum("trkb,tr->tkb", tiled * tiled, curvature, precision=HIGH)
    stacked = jnp.stack([grad_tiles, hess_tiles]).reshape(2, -1, block_width)
    flat_ids = block_ids.reshape(-1)
    stats = jnp.zeros((2, shard_blocks, block_width), jnp.float32).at[:, flat_ids].add(stacked)
    totals = lax.psum(stats, "sample")
    new_weights = newton_update(fixed_weights, totals[0], totals[1])
    fixed_score = partial_margin(tiled, block_ids, new_weights)
    sample_count = lax.axis_size("sample")
    feature_count = lax.axis_size("feature")
    device_count = sample_count * feature_count
    rows_sample = labels.shape[0]
    send_rows = member_feats.shape[0]
    feat_width = member_feats.shape[1]
    member_count = member_coefs.shape[0]
    capacity = max(2, 2 * rows_sample // (feature_count * device_count))
    slot_total = device_count * capacity
    group = slot_total // member_count
    start_row = lax.axis_index("feature") * send_rows
    own_fixed = lax.dynamic_slice_in_dim(fixed_score, start_row, send_rows, 0)
    own_labels = lax.dynamic_slice_in_dim(labels, start_row, send_rows, 0)
    owner_of = member_ids // member_count
    row_range = jnp.arange(send_rows, dtype=jnp.int32)
    earlier = (owner_of[None, :] == owner_of[:, None]) & (row_range[None, :] < row_range[:, None])
    rank_owner = jnp.sum(earlier.astype(jnp.int32), axis=1)
    send_slots = owner_of * capacity + rank_owner
    local_member = jnp.remainder(member_ids, member_count).astype(jnp.float32)
    extras = jnp.stack([own_fixed, own_labels, local_member], axis=1)
    feat_buffer = jnp.zeros((slot_total, feat_width), jnp.float32).at[send_slots].set(member_feats)
    extra_buffer = (
        jnp.zeros((slot_total, 3), jnp.float32).at[:, 2].set(-1.0).at[send_slots].set(extras)
    )
    got_feats, got_extras = (
        lax.all_to_all(
            feat_buffer.reshape(device_count, capacity, feat_width),
            ("sample", "feature"),
            split_axis=0,
            concat_axis=0,
            tiled=True,
        ),
        lax.all_to_all(
            extra_buffer.reshape(device_count, capacity, 3),
            ("sample", "feature"),
            split_axis=0,
            concat_axis=0,
            tiled=True,
        ),
    )
    rows_feats = got_feats.reshape(slot_total, feat_width)
    rows_extra = got_extras.reshape(slot_total, 3)
    member_local = rows_extra[:, 2].astype(jnp.int32)
    sort_key = jnp.where(member_local >= 0, member_local, member_count)
    positions = jnp.arange(slot_total, dtype=jnp.int32)
    order = jnp.argsort(sort_key * slot_total + positions)
    sorted_member = sort_key[order]
    member_range = jnp.arange(member_count, dtype=jnp.int32)
    counts = jnp.sum((sort_key[:, None] == member_range[None, :]).astype(jnp.int32), axis=0)
    offsets = jnp.cumsum(counts) - counts
    clipped = jnp.minimum(sorted_member, member_count - 1)
    rank_in = positions - offsets[clipped]
    target = jnp.where(
        sorted_member < member_count, sorted_member * group + rank_in, member_count * group
    )
    grouped_rows = (
        jnp.full((member_count * group,), slot_total, jnp.int32).at[target].set(order, mode="drop")
    )
    padded_feats = jnp.concatenate([rows_feats, jnp.zeros((1, feat_width), jnp.float32)], axis=0)
    padded_extra = jnp.concatenate([rows_extra, jnp.zeros((1, 3), jnp.float32)], axis=0)
    group_feats = padded_feats[grouped_rows].reshape(member_count, group, feat_width)
    group_extra = padded_extra[grouped_rows].reshape(member_count, group, 3)
    live = (grouped_rows < slot_total).astype(jnp.float32).reshape(member_count, group)
    coefs = member_coefs
    for sweep in range(NEWTON):
        score = jnp.einsum("mgf,mf->mg", group_feats, coefs, precision=HIGH) + group_extra[:, :, 0]
        prob_now = jax.nn.sigmoid(score)
        error = (prob_now - group_extra[:, :, 1]) * live
        weight = prob_now * (1.0 - prob_now) * live
        gradient_re = (
            jnp.einsum("mgf,mg->mf", group_feats, error, precision=HIGH) + MEMBER_RIDGE * coefs
        )
        coefs = coefs - MEMBER_STEP * member_solve(group_feats, weight, gradient_re)
    group_final = jnp.einsum("mgf,mf->mg", group_feats, coefs, precision=HIGH) * live
    final = (
        jnp.zeros((slot_total + 1,), jnp.float32)
        .at[grouped_rows]
        .set(group_final.reshape(-1))[:slot_total]
    )
    returned = lax.all_to_all(
        final.reshape(device_count, capacity),
        ("sample", "feature"),
        split_axis=0,
        concat_axis=0,
        tiled=True,
    )
    member_score = returned.reshape(-1)[send_slots]
    total = own_fixed + member_score
    return (new_weights, coefs, total[:, None])


def solution(mesh):
    in_specs = (
        P("sample", "feature"),
        P("sample", "feature"),
        P("feature", None),
        P("sample"),
        P("sample"),
        P(("sample", "feature"), None),
        P(("sample", "feature")),
        P(("sample", "feature"), None),
    )
    out_specs = (P("feature", None), P(("sample", "feature"), None), P(("sample", "feature"), None))
    return jax.shard_map(shards, mesh=mesh, in_specs=in_specs, out_specs=out_specs, check_vma=False)
```

profile of v0, /device:TPU:1, one launch (start us, length us, event | category | flops | bytes accessed | tf_op | source)
XLA Modules:
  0.0 548.5 jit_solution(9729989409527750932)
XLA Ops:
  7.2 0.7 compare_select_fusion.7
  7.9 0.8 copy.89
  8.7 5.2 reshape.245
  14.1 6.7 %mul.86 = f32[16,128,4,128]{3,2,1,0:T(4,128)} multiply(f32[16,128,4,128]{3,2,1,0:T(4,128)} %reshape.245, f32[16,128,4,128]{3,2,1,0:T(4,128)} %reshape.245) | non-fusion elementwise | flops 1048576 | bytes 12582912 | tf_op jit(solution)/shard_map/mul | solution.py:61
  20.8 2.8 gather_fusion
  23.6 5.7 %fusion.6 = f32[16,1,128,1]{2,1,3,0:T(1,128)S(1)} fusion(f32[16,4,128,1]{2,3,1,0:T(1,128)S(1)} %bitcast.279, f32[16,128,4,128]{3,2,1,0:T(4,128)} %reshape.245), kind=kOutput, calls=%fused_computation.19 | convolution fusion | flops 12582912 | bytes 4235264 | tf_op jit(solution)/shard_map/trkb,tkb->tr/dot_general | solution.py:16
  29.3 9.7 %psum.21 = f32[2048]{0:T(1024)S(1)} all-reduce(f32[2048]{0:T(1024)S(1)} %bitcast.295), channel_id=1, replica_groups=mesh['sample'=32,'feature'=4] {'feature'}, use_global_device_ids=true, to_apply=%region_0.0 | all-reduce | flops 2048 | bytes 16384 | tf_op jit(solution)/shard_map/psum | solution.py:17
  39.0 4.3 fusion.2
  43.4 4.4 fusion
  47.9 5.5 %broadcast_in_dim.31 = f32[2,8192,128]{2,0,1:T(2,128)} broadcast(f32[]{:T(128)} %constant.124.clone.1), dimensions={} | broadcast | bytes 8388612 | tf_op jit(solution)/shard_map/broadcast_in_dim | solution.py:64
  53.4 6.7 %scatter_fusion = f32[2,8192,128]{2,0,1:T(2,128)} fusion(f32[2,8192,128]{2,0,1:T(2,128)} %broadcast_in_dim.31, s32[64]{0:T(128)S(1)} %fusion.52, f32[64,2,128]{2,1,0:T(2,128)S(1)} %maximum_bitcast_fusion), kind=kCustom, calls=%fused_computation.6 | custom fusion | flops 16384 | bytes 196864 | tf_op jit(solution)/shard_map/scatter-add | solution.py:64
  60.2 0.7 copy-done.5
  61.1 2.9 scatter_custom_fusion.1
  64.0 10.3 %all-to-all-start = ((f32[128,8,128]{2,1,0:T(8,128)}), f32[128,8,128]{2,1,0:T(8,128)S(1)}, u32[]{:S(2)}, u32[]{:S(2)}) async-start(f32[128,8,128]{2,1,0:T(8,128)} %bitcast.22), calls=%async_computation | async-start | bytes 1048576 | tf_op jit(solution)/shard_map/all_to_all | solution.py:93
  74.4 113.8 %all-reduce.4.cloned.1.call-done = f32[2,8192,128]{2,0,1:T(2,128)} async-done(((f32[2,8192,128]{2,0,1:T(2,128)}), f32[2,8192,128]{2,0,1:T(2,128)}) %all-reduce.4.cloned.1.call-update) | async-done | bytes 8388624 | tf_op jit(solution)/shard_map/psum | solution.py:65
  188.1 10.6 %fusion.54 = (f32[1,8192,128]{2,0,1:T(1,128)S(1)}, f32[1,8192,128]{2,0,1:T(1,128)S(1)}) fusion(f32[2,8192,128]{2,0,1:T(2,128)} %all-reduce.4.cloned.1.call-done), kind=kLoop, calls=%fused_computation.155 | loop fusion | flops 1048576 | bytes 16777216 | tf_op jit(solution)/shard_map/slice | solution.py:66
  198.8 2.8 divide_subtract_fusion
  201.6 2.8 gather_fusion.1
  204.4 5.7 %fusion.4 = f32[16,1,128,1]{2,1,3,0:T(1,128)S(1)} fusion(f32[16,4,128,1]{2,3,1,0:T(1,128)S(1)} %bitcast.278, f32[16,128,4,128]{3,2,1,0:T(4,128)} %reshape.245), kind=kOutput, calls=%fused_computation.17 | convolution fusion | flops 12582912 | bytes 4235264 | tf_op jit(solution)/shard_map/trkb,tkb->tr/dot_general | solution.py:16
  210.1 8.5 %psum.23 = f32[2048]{0:T(1024)S(1)} all-reduce(f32[2048]{0:T(1024)S(1)} %bitcast.294), channel_id=1, replica_groups=mesh['sample'=32,'feature'=4] {'feature'}, use_global_device_ids=true, to_apply=%region_5.6 | all-reduce | flops 2048 | bytes 16384 | tf_op jit(solution)/shard_map/psum | solution.py:17
  219.0 1.9 scatter_fusion.1
  220.9 1.5 copy.93
  222.4 7.5 %all-to-all-start.1 = ((f32[128,8,3]{1,2,0:T(4,128)}), f32[128,8,3]{1,2,0:T(4,128)S(1)}, u32[]{:S(2)}, u32[]{:S(2)}) async-start(f32[128,8,3]{1,2,0:T(4,128)} %copy.93), calls=%async_computation.1 | async-start | bytes 524288 | tf_op jit(solution)/shard_map/all_to_all | solution.py:100
  229.9 11.3 %all-to-all-done.1 = f32[128,8,3]{1,2,0:T(4,128)S(1)} async-done(((f32[128,8,3]{1,2,0:T(4,128)}), f32[128,8,3]{1,2,0:T(4,128)S(1)}, u32[]{:S(2)}, u32[]{:S(2)}) %all-to-all-start.1) | async-done | bytes 12320 | tf_op jit(solution)/shard_map/all_to_all | solution.py:100
  241.2 0.8 copy.94
  242.0 0.5 fusion.9
  242.9 0.7 fusion.57
  243.6 0.7 fusion.56
  244.4 4.4 sort.17
  248.8 4.5 gather_fusion.2
  253.6 3.5 compare_reduce_fusion.24
  257.1 4.7 select_reduce_fusion.2
  261.8 15.7 %select_select_fusion = s32[1024]{0:T(1024)S(1)} fusion(pred[1024]{0:T(1024)(128)(4,1)S(1)} %get-tuple-element.46, pred[1024]{0:T(1024)(128)(4,1)S(1)} %get-tuple-element.23, pred[1024]{0:T(1024)(128)(4,1)S(1)} %get-tuple-element.28, pred[1024]{0:T(1024)(128)(4,1)S(1)} %get-tuple-element.27, pred[1024]{0:T(1024)(128)(4,1)S(1)} %get-tuple-element.26, ...), kind=kLoop, calls=%fused_computation.132 | loop fusion | flops 25600 | bytes 33892 | tf_op jit(solution)/shard_map/gather | solution.py:119
  278.4 4.5 scatter_custom_fusion.3
  282.9 2.8 gather_fusion.4
  286.5 2.8 gather_fusion.3
  289.4 0.9 fusion.58
  290.4 0.6 fusion.59
  290.9 1.0 convolution_bitcast_fusion.5
  291.9 1.2 convolution_add_fusion.1
  293.4 93.8 %custom-call.12 = f32[32,32,32]{2,1,0:T(8,128)S(1)} custom-call(f32[32,32,32]{2,1,0:T(8,128)S(1)} %fusion.12), custom_call_target="Cholesky" | custom-call | tf_op jit(solution)/shard_map/jit(cholesky)/cholesky | solution.py:33
  388.0 12.5 %custom-call.14 = f32[32,1,32,32]{0,2,3,1:T(8,128)S(1)} custom-call(f32[32,1,32,32]{0,3,2,1:T(8,128)S(1)} %select_bitcast_fusion.1), custom_call_target="InvertDiagBlocksLowerTriangular" | custom-call | tf_op jit(solution)/shard_map/triangular_solve/custom-call.2 | solution.py:35
  400.4 0.4 copy.134
  400.9 0.6 convolution_bitcast_fusion.4
  401.5 0.9 convolution_bitcast_fusion.3
  402.4 0.7 fusion.18
  403.1 0.9 fusion.60
  404.0 0.6 fusion.61
  404.6 1.2 convolution_add_fusion
  405.8 1.0 convolution_bitcast_fusion.2
  407.1 93.8 %custom-call.15 = f32[32,32,32]{2,1,0:T(8,128)S(1)} custom-call(f32[32,32,32]{2,1,0:T(8,128)S(1)} %fusion.11), custom_call_target="Cholesky" | custom-call | tf_op jit(solution)/shard_map/jit(cholesky)/cholesky | solution.py:33
  501.6 12.7 %custom-call.17 = f32[32,1,32,32]{0,2,3,1:T(8,128)S(1)} custom-call(f32[32,1,32,32]{0,3,2,1:T(8,128)S(1)} %select_bitcast_fusion), custom_call_target="InvertDiagBlocksLowerTriangular" | custom-call | tf_op jit(solution)/shard_map/triangular_solve/custom-call.2 | solution.py:35
  514.8 0.6 convolution_bitcast_fusion.1
  515.4 0.9 convolution_bitcast_fusion
  516.3 0.7 fusion.14
  517.0 0.9 fusion.62
  518.0 4.3 scatter_custom_fusion.4
  522.4 0.7 all_to_all.14
  523.1 3.9 all-to-all-start.2
  527.0 9.9 %all-to-all-done.2 = f32[128,1,8]{2,1,0:T(1,128)S(1)} async-done(((f32[128,1,8]{2,1,0:T(1,128)}), f32[128,1,8]{2,1,0:T(1,128)S(1)}, u32[]{:S(2)}, u32[]{:S(2)}) %all-to-all-start.2) | async-done | bytes 4128 | tf_op jit(solution)/shard_map/all_to_all | solution.py:147
  536.8 0.5 broadcast.608
  537.4 0.8 reduce.68
  538.3 2.3 gather_fusion.5
  540.6 0.7 dynamic-slice_add_fusion
  (80 shorter events, 6.2 us)
Async XLA Ops:
  7.2 181.0 %all-reduce.4.cloned.1.call-start = ((), (), s32[]{:S(2)}) async-start(), calls=%async_computation.3 | async-start | bytes 16777216 | tf_op jit(solution)/shard_map/psum | solution.py:65
  20.8 18.2 %copy-start.3 = (f32[2048]{0:T(1024)S(1)}, f32[2048]{0:T(1024)}, u32[]{:S(2)}) copy-start(f32[2048]{0:T(1024)} %param.18) | copy-start | bytes 24580
  20.8 18.2 %copy-start.4 = (f32[2048]{0:T(1024)S(1)}, f32[2048]{0:T(1024)}, u32[]{:S(2)}) copy-start(f32[2048]{0:T(1024)} %param.19) | copy-start | bytes 24580
  60.1 0.7 copy-start.5
  64.0 158.4 %all-to-all-start = ((f32[128,8,128]{2,1,0:T(8,128)}), f32[128,8,128]{2,1,0:T(8,128)S(1)}, u32[]{:S(2)}, u32[]{:S(2)}) async-start(f32[128,8,128]{2,1,0:T(8,128)} %bitcast.22), calls=%async_computation | async-start | bytes 1048576 | tf_op jit(solution)/shard_map/all_to_all | solution.py:93
  188.1 10.6 %copy-start = (f32[8192,128]{1,0:T(8,128)S(1)}, f32[8192,128]{1,0:T(8,128)}, u32[]{:S(2)}) copy-start(f32[8192,128]{1,0:T(8,128)} %param.17) | copy-start | bytes 12582916
  201.6 17.3 %copy-start.6 = (f32[3]{0:T(128)S(1)}, f32[3]{0:T(128)}, u32[]{:S(2)}) copy-start(f32[3]{0:T(128)} %constant.136.clone.1) | copy-start | bytes 40
  222.4 18.8 %all-to-all-start.1 = ((f32[128,8,3]{1,2,0:T(4,128)}), f32[128,8,3]{1,2,0:T(4,128)S(1)}, u32[]{:S(2)}, u32[]{:S(2)}) async-start(f32[128,8,3]{1,2,0:T(4,128)} %copy.93), calls=%async_computation.1 | async-start | bytes 524288 | tf_op jit(solution)/shard_map/all_to_all | solution.py:100
  285.7 3.6 copy-start.1
  517.0 24.2 %copy-start.2 = (f32[32,128]{1,0:T(8,128)}, f32[32,128]{1,0:T(8,128)S(1)}, u32[]{:S(2)}) copy-start(f32[32,128]{1,0:T(8,128)S(1)} %multiply_subtract_fusion) | copy-start | bytes 49156
  523.1 13.8 %all-to-all-start.2 = ((f32[128,1,8]{2,1,0:T(1,128)}), f32[128,1,8]{2,1,0:T(1,128)S(1)}, u32[]{:S(2)}, u32[]{:S(2)}) async-start(f32[128,1,8]{2,1,0:T(1,128)} %bitcast.149), calls=%async_computation.2 | async-start | bytes 131072 | tf_op jit(solution)/shard_map/all_to_all | solution.py:147
Sparse Core Ops, SparseCore 0:
  60.3 127.7 all-reduce.3
where the time goes:
time: 558 us; the launch traced here: 549 us
  other arithmetic  273 us (49%)
  waiting for transfers between devices  135 us (24%)
  local copies, waits for them, and re-layouts  53.2 us (10%)
  matrix products  32.7 us (6%)
  starting transfers between devices  21.7 us (4%)
  blocking collectives  18.2 us (3%)
  between operations  15 us (3%)
    another operation x7, other arithmetic, member_solve(): factor = jnp.linalg.cholesky(small)  188 us
    psum x1, waiting for transfers between devices, shards(): totals = lax.psum(stats, 'sample')  114 us
    another operation x5, other arithmetic, member_solve(): lax.linalg.triangular_solve(factor, middle, left_side=True, lower=True, t...  25.6 us
    gather x3, other arithmetic, shards(): rank_in = positions - offsets[clipped]  23.9 us
    psum x2, blocking collectives, partial_margin(): return lax.psum(local, 'feature')  18.2 us
    dot_general x2, matrix products, partial_margin(): jnp.einsum('trkb,tkb->tr', tiled, chosen, precision=HIGH).reshape(-1)  11.4 us
    all_to_all x1, waiting for transfers between devices, shards(): lax.all_to_all(extra_buffer.reshape(device_count, capacity, 3), ('sample'...  11.3 us
  transfers between devices with their start and end apart: 4, of which 3 were waited for; matrix products, arithmetic and copies ran while one was open for 5% of the time, Pallas kernels for 0%

commit v1 on v0

--- a/solution.py
+++ b/solution.py
@@ -62,7 +62,9 @@
     stacked = jnp.stack([grad_tiles, hess_tiles]).reshape(2, -1, block_width)
     flat_ids = block_ids.reshape(-1)
     stats = jnp.zeros((2, shard_blocks, block_width), jnp.float32).at[:, flat_ids].add(stacked)
-    totals = lax.psum(stats, "sample")
+    totals = stats
+    for hop in (1, 2, 4, 8, 16):
+        totals = totals + lax.ppermute(totals, "sample", [(dev, dev ^ hop) for dev in range(32)])
     new_weights = newton_update(fixed_weights, totals[0], totals[1])
     fixed_score = partial_margin(tiled, block_ids, new_weights)
     sample_count = lax.axis_size("sample")

time: 558 us -> 1190 us (2.13)
  waiting for transfers between devices: 135 us -> 740 us
  other arithmetic: 273 us -> 297 us
  starting transfers between devices: 21.7 us -> 39.8 us
  between operations: 15 us -> 1.41 us
    ppermute x0 -> x5, waiting for transfers between devices: none -> 719 us  [shards(): lax.ppermute(totals, 'sample', [(dev, dev ^ hop) for dev in range(32)])]
    psum x1 -> x0, waiting for transfers between devices: 114 us -> none  [shards(): totals = lax.psum(stats, 'sample')]
    add x0 -> x5, other arithmetic: none -> 27.6 us  [shards(): totals + lax.ppermute(totals, 'sample', [(dev, dev ^ hop) for dev in rang...]
  transfers between devices with their start and end apart: 4 -> 8, of which waited for: 3 -> 7; matrix products, arithmetic and copies ran while one was open for 5% -> 3% of each run, Pallas kernels for 0% -> 0%
where the time goes in v1:
time: 1190 us; the launch traced here: 1180 us
  waiting for transfers between devices  740 us (62%)
  other arithmetic  297 us (25%)
  local copies, waits for them, and re-layouts  52.5 us (4%)
  starting transfers between devices  39.8 us (3%)
  matrix products  32.7 us (3%)
  blocking collectives  15.7 us (1%)
    ppermute x5, waiting for transfers between devices, shards(): lax.ppermute(totals, 'sample', [(dev, dev ^ hop) for dev in range(32)])  719 us
    another operation x7, other arithmetic, member_solve(): factor = jnp.linalg.cholesky(small)  188 us
    add x5, other arithmetic, shards(): totals + lax.ppermute(totals, 'sample', [(dev, dev ^ hop) for dev in rang...  27.6 us
    another operation x5, other arithmetic, member_solve(): lax.linalg.triangular_solve(factor, middle, left_side=True, lower=True, t...  25.8 us
    gather x3, other arithmetic, shards(): rank_in = positions - offsets[clipped]  23.9 us
  transfers between devices with their start and end apart: 8, of which 7 were waited for; matrix products, arithmetic and copies ran while one was open for 3% of the time, Pallas kernels for 0%

profile of v1, /device:TPU:1, one launch (start us, length us, event | category | flops | bytes accessed | tf_op | source)
XLA Modules:
  0.0 1178.8 jit_solution(17018707260870122470)
XLA Ops:
  1.3 0.8 copy.89
  2.1 5.2 reshape.245
  7.5 6.7 mul.86
  14.2 2.8 gather_fusion
  17.1 5.7 fusion.6
  22.8 9.7 psum.14
  32.5 4.3 fusion.2
  36.9 4.4 fusion
  41.4 5.4 broadcast_in_dim.31
  46.8 6.7 scatter_fusion
  53.4 2.7 collective-permute-start
  56.1 13.0 %collective-permute-done = f32[2,8192,128]{2,0,1:T(2,128)S(1)} collective-permute-done((f32[2,8192,128]{2,0,1:T(2,128)}, f32[2,8192,128]{2,0,1:T(2,128)S(1)}, u32[]{:S(2)}, u32[]{:S(2)}) %collective-permute-start) | collective-permute-done | bytes 8388640 | tf_op jit(solution)/shard_map/ppermute | solution.py:67
  69.1 6.1 add.173
  75.2 1.7 collective-permute-start.1
  76.9 180.4 %collective-permute-done.1 = f32[2,8192,128]{2,0,1:T(2,128)S(1)} collective-permute-done((f32[2,8192,128]{2,0,1:T(2,128)S(1)}, f32[2,8192,128]{2,0,1:T(2,128)S(1)}, u32[]{:S(2)}, u32[]{:S(2)}) %collective-permute-start.1) | collective-permute-done | bytes 8388640 | tf_op jit(solution)/shard_map/ppermute | solution.py:67
  257.4 4.4 add.174
  261.8 3.4 collective-permute-start.2
  265.2 179.6 %collective-permute-done.2 = f32[2,8192,128]{2,0,1:T(2,128)S(1)} collective-permute-done((f32[2,8192,128]{2,0,1:T(2,128)S(1)}, f32[2,8192,128]{2,0,1:T(2,128)S(1)}, u32[]{:S(2)}, u32[]{:S(2)}) %collective-permute-start.2) | collective-permute-done | bytes 8388640 | tf_op jit(solution)/shard_map/ppermute | solution.py:67
  444.8 4.4 add.175
  449.2 1.3 collective-permute-start.3
  450.6 178.9 %collective-permute-done.3 = f32[2,8192,128]{2,0,1:T(2,128)S(1)} collective-permute-done((f32[2,8192,128]{2,0,1:T(2,128)S(1)}, f32[2,8192,128]{2,0,1:T(2,128)S(1)}, u32[]{:S(2)}, u32[]{:S(2)}) %collective-permute-start.3) | collective-permute-done | bytes 8388640 | tf_op jit(solution)/shard_map/ppermute | solution.py:67
  629.4 5.4 add.176
  634.9 2.7 collective-permute-start.4
  637.9 2.9 scatter_custom_fusion.1
  640.8 7.9 all-to-all-start
  648.8 167.2 %collective-permute-done.4 = f32[2,8192,128]{2,0,1:T(2,128)} collective-permute-done((f32[2,8192,128]{2,0,1:T(2,128)}, f32[2,8192,128]{2,0,1:T(2,128)}, u32[]{:S(2)}, u32[]{:S(2)}) %collective-permute-start.4) | collective-permute-done | bytes 8388640 | tf_op jit(solution)/shard_map/ppermute | solution.py:67
  815.9 7.2 add.177
  823.2 6.6 fusion.54
  829.8 2.8 divide_subtract_fusion
  832.7 2.8 gather_fusion.1
  835.5 5.7 fusion.4
  841.2 6.1 psum.15
  847.6 1.9 scatter_fusion.1
  849.5 1.5 copy.93
  851.0 16.2 %all-to-all-start.1 = ((f32[128,8,3]{1,2,0:T(4,128)}), f32[128,8,3]{1,2,0:T(4,128)S(1)}, u32[]{:S(2)}, u32[]{:S(2)}) async-start(f32[128,8,3]{1,2,0:T(4,128)} %copy.93), calls=%async_computation.1 | async-start | bytes 524288 | tf_op jit(solution)/shard_map/all_to_all | solution.py:102
  867.2 11.1 all-to-all-done.1
  878.4 0.8 copy.94
  880.8 0.7 fusion.56
  881.6 4.4 sort.17
  886.0 4.5 gather_fusion.2
  890.8 3.5 compare_reduce_fusion.24
  894.3 4.7 select_reduce_fusion.2
  899.0 15.7 %select_select_fusion = s32[1024]{0:T(1024)S(1)} fusion(pred[1024]{0:T(1024)(128)(4,1)S(1)} %get-tuple-element.46, pred[1024]{0:T(1024)(128)(4,1)S(1)} %get-tuple-element.23, pred[1024]{0:T(1024)(128)(4,1)S(1)} %get-tuple-element.28, pred[1024]{0:T(1024)(128)(4,1)S(1)} %get-tuple-element.27, pred[1024]{0:T(1024)(128)(4,1)S(1)} %get-tuple-element.26, ...), kind=kLoop, calls=%fused_computation.132 | loop fusion | flops 25600 | bytes 33892 | tf_op jit(solution)/shard_map/gather | solution.py:121
  915.6 4.6 scatter_custom_fusion.3
  920.2 2.8 gather_fusion.4
  923.7 2.8 gather_fusion.3
  926.6 0.9 fusion.58
  928.2 1.0 convolution_bitcast_fusion.5
  929.2 1.2 convolution_add_fusion.1
  930.7 93.8 %custom-call.12 = f32[32,32,32]{2,1,0:T(8,128)S(1)} custom-call(f32[32,32,32]{2,1,0:T(8,128)S(1)} %fusion.12), custom_call_target="Cholesky" | custom-call | tf_op jit(solution)/shard_map/jit(cholesky)/cholesky | solution.py:33
  1025.2 12.5 %custom-call.14 = f32[32,1,32,32]{0,2,3,1:T(8,128)S(1)} custom-call(f32[32,1,32,32]{0,3,2,1:T(8,128)S(1)} %select_bitcast_fusion.1), custom_call_target="InvertDiagBlocksLowerTriangular" | custom-call | tf_op jit(solution)/shard_map/triangular_solve/custom-call.2 | solution.py:35
  1038.7 0.9 convolution_bitcast_fusion.3
  1040.3 0.9 fusion.60
  1041.9 1.2 convolution_add_fusion
  1043.0 1.0 convolution_bitcast_fusion.2
  1044.3 93.8 %custom-call.15 = f32[32,32,32]{2,1,0:T(8,128)S(1)} custom-call(f32[32,32,32]{2,1,0:T(8,128)S(1)} %fusion.11), custom_call_target="Cholesky" | custom-call | tf_op jit(solution)/shard_map/jit(cholesky)/cholesky | solution.py:33
  1138.9 12.9 %custom-call.17 = f32[32,1,32,32]{0,2,3,1:T(8,128)S(1)} custom-call(f32[32,1,32,32]{0,3,2,1:T(8,128)S(1)} %select_bitcast_fusion), custom_call_target="InvertDiagBlocksLowerTriangular" | custom-call | tf_op jit(solution)/shard_map/triangular_solve/custom-call.2 | solution.py:35
  1152.8 0.9 convolution_bitcast_fusion
  1154.5 0.9 fusion.62
  1155.5 4.3 scatter_custom_fusion.4
  1160.5 3.9 all-to-all-start.2
  1164.4 9.9 all-to-all-done.2
  1174.8 0.8 reduce.68
  1175.7 2.3 gather_fusion.5
  (92 shorter events, 14.0 us)
Async XLA Ops:
  14.2 18.2 %copy-start.3 = (f32[2048]{0:T(1024)S(1)}, f32[2048]{0:T(1024)}, u32[]{:S(2)}) copy-start(f32[2048]{0:T(1024)} %param.18) | copy-start | bytes 24580
  14.2 18.2 %copy-start.4 = (f32[2048]{0:T(1024)S(1)}, f32[2048]{0:T(1024)}, u32[]{:S(2)}) copy-start(f32[2048]{0:T(1024)} %param.19) | copy-start | bytes 24580
  53.4 15.7 %collective-permute-start = (f32[2,8192,128]{2,0,1:T(2,128)}, f32[2,8192,128]{2,0,1:T(2,128)S(1)}, u32[]{:S(2)}, u32[]{:S(2)}) collective-permute-start(f32[2,8192,128]{2,0,1:T(2,128)} %scatter_fusion), channel_id=1, source_target_pairs={{0,4},{4,0},{8,12},{12,8},{16,20},{20,16},{24,28},{28,24},{32,36},... | collective-permute-start | bytes 25165832 | tf_op jit(solution)/shard_map/ppermute | solution.py:67
  75.2 182.2 %collective-permute-start.1 = (f32[2,8192,128]{2,0,1:T(2,128)S(1)}, f32[2,8192,128]{2,0,1:T(2,128)S(1)}, u32[]{:S(2)}, u32[]{:S(2)}) collective-permute-start(f32[2,8192,128]{2,0,1:T(2,128)S(1)} %add.173), channel_id=1, source_target_pairs={{0,8},{4,12},{8,0},{12,4},{16,24},{20,28},{24,16},{28,20},{32,40},... | collective-permute-start | bytes 25165832 | tf_op jit(solution)/shard_map/ppermute | solution.py:67
  261.8 183.0 %collective-permute-start.2 = (f32[2,8192,128]{2,0,1:T(2,128)S(1)}, f32[2,8192,128]{2,0,1:T(2,128)S(1)}, u32[]{:S(2)}, u32[]{:S(2)}) collective-permute-start(f32[2,8192,128]{2,0,1:T(2,128)S(1)} %add.174), channel_id=1, source_target_pairs={{0,16},{4,20},{8,24},{12,28},{16,0},{20,4},{24,8},{28,12},{32,48},... | collective-permute-start | bytes 25165832 | tf_op jit(solution)/shard_map/ppermute | solution.py:67
  449.2 188.4 %copy-start.5 = (s32[512]{0:T(512)S(1)}, s32[512]{0:T(512)}, u32[]{:S(2)}) copy-start(s32[512]{0:T(512)} %param.21) | copy-start | bytes 6148
  449.2 180.2 %collective-permute-start.3 = (f32[2,8192,128]{2,0,1:T(2,128)S(1)}, f32[2,8192,128]{2,0,1:T(2,128)S(1)}, u32[]{:S(2)}, u32[]{:S(2)}) collective-permute-start(f32[2,8192,128]{2,0,1:T(2,128)S(1)} %add.175), channel_id=1, source_target_pairs={{0,32},{4,36},{8,40},{12,44},{16,48},{20,52},{24,56},{28,60},{32,0... | collective-permute-start | bytes 25165832 | tf_op jit(solution)/shard_map/ppermute | solution.py:67
  634.9 181.1 %collective-permute-start.4 = (f32[2,8192,128]{2,0,1:T(2,128)}, f32[2,8192,128]{2,0,1:T(2,128)}, u32[]{:S(2)}, u32[]{:S(2)}) collective-permute-start(f32[2,8192,128]{2,0,1:T(2,128)} %add.176), channel_id=1, source_target_pairs={{0,64},{4,68},{8,72},{12,76},{16,80},{20,84},{24,88},{28,92},{32,9... | collective-permute-start | bytes 25165832 | tf_op jit(solution)/shard_map/ppermute | solution.py:67
  640.8 210.3 %all-to-all-start = ((f32[128,8,128]{2,1,0:T(8,128)}), f32[128,8,128]{2,1,0:T(8,128)S(1)}, u32[]{:S(2)}, u32[]{:S(2)}) async-start(f32[128,8,128]{2,1,0:T(8,128)} %bitcast.22), calls=%async_computation | async-start | bytes 1048576 | tf_op jit(solution)/shard_map/all_to_all | solution.py:95
  823.2 6.6 copy-start
  832.7 14.9 %copy-start.6 = (f32[3]{0:T(128)S(1)}, f32[3]{0:T(128)}, u32[]{:S(2)}) copy-start(f32[3]{0:T(128)} %constant.136.clone.1) | copy-start | bytes 40
  851.0 27.4 %all-to-all-start.1 = ((f32[128,8,3]{1,2,0:T(4,128)}), f32[128,8,3]{1,2,0:T(4,128)S(1)}, u32[]{:S(2)}, u32[]{:S(2)}) async-start(f32[128,8,3]{1,2,0:T(4,128)} %copy.93), calls=%async_computation.1 | async-start | bytes 524288 | tf_op jit(solution)/shard_map/all_to_all | solution.py:102
  923.0 3.6 copy-start.1
  1154.5 24.2 %copy-start.2 = (f32[32,128]{1,0:T(8,128)}, f32[32,128]{1,0:T(8,128)S(1)}, u32[]{:S(2)}) copy-start(f32[32,128]{1,0:T(8,128)S(1)} %multiply_subtract_fusion) | copy-start | bytes 49156
  1160.5 13.8 %all-to-all-start.2 = ((f32[128,1,8]{2,1,0:T(1,128)}), f32[128,1,8]{2,1,0:T(1,128)S(1)}, u32[]{:S(2)}, u32[]{:S(2)}) async-start(f32[128,1,8]{2,1,0:T(1,128)} %bitcast.149), calls=%async_computation.2 | async-start | bytes 131072 | tf_op jit(solution)/shard_map/all_to_all | solution.py:149
